TPU v7x, 256 devices: a whole 4x4x8 slice. The times are simulated.
256 devices in a mesh: fsdp: 64 (over x, z, core), rep: 4 (over y).
Axes of the slice: x: 4, y: 4, z: 8, core: 2. Of those that a mesh axis runs over, the one named last changes fastest.
Arguments:
- grad: float32 [4, 256, 65536], P('rep', 'fsdp'), may hold values from -45 to 45
- z_params: float32 [4, 256, 65536], P('rep', 'fsdp'), may hold values from -6 to 6
- x_params: float32 [4, 256, 65536], P('rep', 'fsdp'), may hold values from -6 to 6
- owner: int32 [64], replicated, may hold values from 0 to 63, each once
- stat_left: float32 [64, 1024, 1024], P('fsdp', 'rep'), may hold values from -6 to 6
- stat_right: float32 [64, 1024, 1024], P('fsdp', 'rep'), may hold values from -6 to 6
- root_left: bfloat16 [64, 1024, 1024], P('fsdp', 'rep'), may hold values from -0.1875 to 0.1875
- root_right: bfloat16 [64, 1024, 1024], P('fsdp', 'rep'), may hold values from -0.1875 to 0.1875
Outputs:
- z_new: float32 [4, 256, 65536], P('rep', 'fsdp')
- x_new: float32 [4, 256, 65536], P('rep', 'fsdp')
- y_new: bfloat16 [4, 256, 65536], P('rep', 'fsdp')
- left_new: float32 [64, 1024, 1024], P('fsdp', 'rep')
- right_new: float32 [64, 1024, 1024], P('fsdp', 'rep')
Inputs may be any that keep to these rules, and one draw needn't show every extreme that they name: `owner`: each fsdp index owns exactly one block.
All inputs are finite; a program needn't handle non-finite values.
Results may differ from a plain program's by a relative error of at most 0.0025.
Values may be sent and summed in bfloat16 or wider, within the bound.
A program may use at most 320 MiB of HBM per device.

v0:
```python
import jax
import jax.numpy as jnp
from jax import lax
from jax.sharding import PartitionSpec as P


def accumulate(carry, piece, start, own_rows, root_rows, member_start):
    left_part, right_part, product, squares = carry
    columns = jnp.dot(own_rows, piece.T, precision=lax.Precision.HIGHEST)
    left_part = lax.dynamic_update_slice_in_dim(left_part, columns, start, 1)
    strip = lax.dynamic_slice_in_dim(piece, member_start, own_rows.shape[0], 1)
    right_part = right_part + jnp.dot(strip.T, piece, precision=lax.Precision.HIGHEST)
    product = jnp.dot(root_rows, piece.astype(jnp.bfloat16), preferred_element_type=jnp.float32)
    squares = squares + jnp.sum(piece * piece)
    return (left_part, right_part, product, squares)


def per_device(grad, z_params, x_params, owner, stat_left, stat_right, root_left, root_right):
    owners = lax.axis_size("fsdp")
    member = lax.axis_index("rep")
    block_size = stat_left.shape[2]
    quarter = stat_left.shape[1]
    member_start = member * quarter
    slots = jnp.arange(owners, dtype=jnp.int32)
    matches = (owner[None, :] == slots[:, None]).astype(jnp.int32)
    inverse = jnp.sum(slots[None, :] * matches, axis=1)
    root_rows = root_left[0]
    zero_block = jnp.zeros((quarter, block_size), jnp.float32)
    start_carry = (zero_block, zero_block, zero_block, jnp.zeros((), jnp.float32))
    flat = grad[0]
    ordered = jnp.take(flat.reshape(flat.shape[0], owners, block_size), inverse, axis=1).reshape(
        flat.shape
    )
    own_rows = lax.all_to_all(
        ordered.astype(jnp.bfloat16), "fsdp", split_axis=1, concat_axis=0, tiled=True
    ).astype(ordered.dtype)
    totals = accumulate(
        start_carry,
        lax.all_gather(own_rows.astype(jnp.bfloat16), "rep", axis=0, tiled=True).astype(
            jnp.float32
        ),
        jnp.int32(0),
        own_rows,
        root_rows,
        member_start,
    )
    left_part, right_part, product, squares = totals
    left_new = 0.95 * stat_left[0] + 0.05 / block_size * left_part
    right_new = 0.95 * stat_right[0] + 0.05 / block_size * right_part
    left_prod = product.astype(jnp.bfloat16)
    precond = jnp.dot(
        left_prod,
        lax.all_gather(root_right[0], "rep", axis=0, tiled=True),
        preferred_element_type=jnp.float32,
    )
    direction_sq = lax.psum(jnp.sum(precond * precond), "rep")
    entries = float(block_size * block_size)
    scale = jnp.sqrt(squares / entries) * lax.rsqrt(direction_sq / entries + 1e-06)
    direction = (scale * precond).astype(jnp.bfloat16)
    returned = lax.all_to_all(direction, "fsdp", split_axis=0, concat_axis=1, tiled=True)
    rows_dev = returned.shape[0]
    flat_dir = jnp.take(returned.reshape(rows_dev, owners, block_size), owner, axis=1).reshape(
        z_params.shape
    )
    z_new = z_params - 0.2 * flat_dir.astype(jnp.float32)
    x_new = 0.75 * x_params + 0.25 * z_new
    y_new = (0.1 * z_new + 0.9 * x_new).astype(jnp.bfloat16)
    return (z_new, x_new, y_new, left_new[None], right_new[None])


def solution(mesh):
    return jax.shard_map(
        per_device,
        mesh=mesh,
        in_specs=(
            P("rep", "fsdp", None),
            P("rep", "fsdp", None),
            P("rep", "fsdp", None),
            P(),
            P("fsdp", "rep", None),
            P("fsdp", "rep", None),
            P("fsdp", "rep", None),
            P("fsdp", "rep", None),
        ),
        out_specs=(
            P("rep", "fsdp", None),
            P("rep", "fsdp", None),
            P("rep", "fsdp", None),
            P("fsdp", "rep", None),
            P("fsdp", "rep", None),
        ),
        check_vma=False,
    )
```

profile of v0, /device:TPU:1, one launch (start us, length us, event | category | flops | bytes accessed | tf_op | source)
XLA Modules:
  0.0 167.5 jit_solution(2779815434879150034)
XLA Ops:
  7.2 0.0 copy-start
  7.2 0.0 all-gather.4.cloned.1.call-start
  7.2 0.8 select_reduce_fusion
  8.1 0.3 copy-done
  8.4 1.1 gather_fusion
  9.6 0.0 copy-start.4
  9.6 0.3 fusion.6
  9.9 30.1 %all_to_all.32 = bf16[4,64,1024]{2,0,1:T(4,128)(2,1)S(1)} all-to-all(bf16[4,64,1024]{2,0,1:T(4,128)(2,1)S(1)} %fusion.6), channel_id=1, replica_groups=mesh['fsdp'=64,'rep'=4] {'fsdp'}, dimensions={1} | all-to-all | bytes 1048576 | tf_op jit(solution)/shard_map/all_to_all | solution.py:34
  40.0 0.9 all_to_all.26
  40.9 0.0 all-gather.4.cloned.1.call-update
  40.9 0.0 all-gather.6.cloned.1.call-start
  41.0 0.7 all-gather.6.cloned.1.call-update
  41.7 0.0 copy-done.4
  41.7 29.9 %all-gather.4.cloned.1.call-done = bf16[1024,1024]{1,0:T(8,128)(2,1)} async-done(((bf16[256,1024]{1,0:T(8,128)(2,1)}), bf16[1024,1024]{1,0:T(8,128)(2,1)}) %all-gather.4.cloned.1.call-update) | async-done | bytes 2097168 | tf_op jit(solution)/shard_map/all_gather | solution.py:39
  71.6 0.0 copy-start.1
  71.6 3.4 %multiply_reduce_fusion = f32[]{:T(128)} fusion(bf16[1024,1024]{1,0:T(8,128)(2,1)} %all-gather.4.cloned.1.call-done), kind=kLoop, calls=%fused_computation.2 | loop fusion | flops 3145727 | bytes 2097156 | tf_op jit(solution)/shard_map/reduce_sum | solution.py:14
  75.7 31.2 %all-gather.6.cloned.1.call-done = bf16[1,1024,1024]{2,1,0:T(8,128)(2,1)} async-done(((bf16[1,256,1024]{2,1,0:T(8,128)(2,1)}), bf16[1,1024,1024]{2,1,0:T(8,128)(2,1)}) %all-gather.6.cloned.1.call-update) | async-done | bytes 2097168 | tf_op jit(solution)/shard_map/all_gather | solution.py:53
  106.9 0.0 copy-done.1
  106.9 5.7 %multiply_reduce_fusion.1 = (f32[]{:T(128)}, f32[256,1024]{1,0:T(8,128)}) fusion(bf16[1,1024,1024]{2,1,0:T(8,128)(2,1)} %all-gather.6.cloned.1.call-done, bf16[1024,1024]{1,0:T(8,128)(2,1)S(1)} %copy-done.1, bf16[1,256,1024]{2,1,0:T(8,128)(2,1)} %param.14), kind=kOutput, calls=%fused_computation.17 | convolution fusion | flops 1074528256 | bytes 5767172 | tf_op jit(solution)/shard_map/dot_general | solution.py:51
  112.5 7.2 %psum.7 = f32[]{:T(128)} all-reduce(f32[]{:T(128)} %get-tuple-element.8), channel_id=1, replica_groups=mesh['fsdp'=64,'rep'=4] {'rep'}, use_global_device_ids=true, to_apply=%region_3.4 | all-reduce | flops 1 | bytes 8 | tf_op jit(solution)/shard_map/psum | solution.py:56
  120.4 2.1 %multiply_convert_fusion = bf16[256,1024]{1,0:T(8,128)(2,1)} fusion(f32[256,1024]{1,0:T(8,128)} %get-tuple-element.9, f32[]{:T(128)S(6)} %mul.86), kind=kLoop, calls=%fused_computation.16 | loop fusion | flops 524288 | bytes 1572868 | tf_op jit(solution)/shard_map/convert_element_type | solution.py:59
  122.5 2.0 %all_to_all.27 = bf16[64,4,1024]{2,1,0:T(4,128)(2,1)} reshape(bf16[256,1024]{1,0:T(8,128)(2,1)} %multiply_convert_fusion) | data formatting | bytes 1048576 | tf_op jit(solution)/shard_map/all_to_all | solution.py:60
  124.5 12.9 %all-to-all-start.1 = ((bf16[64,4,1024]{2,1,0:T(4,128)(2,1)}), bf16[64,4,1024]{2,1,0:T(4,128)(2,1)}, u32[]{:S(2)}, u32[]{:S(2)}) async-start(bf16[64,4,1024]{2,1,0:T(4,128)(2,1)} %all_to_all.27), calls=%async_computation.1 | async-start | bytes 1048576 | tf_op jit(solution)/shard_map/all_to_all | solution.py:60
  137.4 0.1 broadcast_bitcast_fusion
  137.6 0.0 copy-start.2
  137.6 0.0 copy-start.3
  137.6 3.1 %fusion.3 = f32[1,256,1024]{2,1,0:T(8,128)} fusion(bf16[1024,1024]{1,0:T(8,128)(2,1)S(1)} %copy-done.1, f32[1,256,1024]{2,1,0:T(8,128)} %param.13, s32[]{:T(128)S(6)} %select_n.46), kind=kOutput, calls=%fused_computation.7 | convolution fusion | flops 537657344 | bytes 4718596 | tf_op jit(solution)/shard_map/dot_general | solution.py:12
  140.7 0.0 copy-done.2
  140.7 0.0 copy-done.3
  140.7 1.8 %fusion.5 = f32[1,256,1024]{2,1,0:T(8,128)} fusion(bf16[256,1024]{1,0:T(8,128)(2,1)S(1)} %copy-done.2, bf16[1024,1024]{1,0:T(8,128)(2,1)S(1)} %copy-done.1, f32[1,256,1024]{2,1,0:T(8,128)S(1)} %copy-done.3), kind=kOutput, calls=%fused_computation.10 | convolution fusion | flops 537657344 | bytes 4718592 | tf_op jit(solution)/shard_map/dot_general | solution.py:9
  142.4 12.2 %all-to-all-done.1 = bf16[64,4,1024]{2,1,0:T(4,128)(2,1)} async-done(((bf16[64,4,1024]{2,1,0:T(4,128)(2,1)}), bf16[64,4,1024]{2,1,0:T(4,128)(2,1)}, u32[]{:S(2)}, u32[]{:S(2)}) %all-to-all-start.1) | async-done | bytes 524320 | tf_op jit(solution)/shard_map/all_to_all | solution.py:60
  154.6 2.0 %gather_fusion.1 = bf16[64,4,1024]{2,1,0:T(4,128)(2,1)S(1)} fusion(bf16[4,64,1024]{2,0,1:T(4,128)(2,1)} %bitcast.7, s32[1024]{0:T(1024)S(1)} %pad_clamp_fusion), kind=kCustom, calls=%fused_computation.1 | custom fusion | bytes 1048832 | tf_op jit(solution)/shard_map/jit(_take)/gather | solution.py:62
  156.7 3.9 %add_convert_fusion = (bf16[1,4,65536]{2,1,0:T(4,128)(2,1)}, f32[1,4,65536]{2,1,0:T(4,128)}, f32[1,4,65536]{2,1,0:T(4,128)}) fusion(f32[1,4,65536]{2,1,0:T(4,128)} %param.10, f32[1,4,65536]{2,1,0:T(4,128)} %param.9, bf16[1,4,65536]{2,1,0:T(4,128)(2,1)S(1)} %bitcast.40, pred[65536]{0:T(1024)(128)(4,1)S(1)} %bitcast.41), kind=kLoop, calls=%fused_computation.13 | loop fusion | flops 2883584 | bytes 5308416 | tf_op jit(solution)/shard_map/convert_element_type | solution.py:67
  (7 shorter events, 0.1 us)
Async XLA Ops:
  7.2 1.2 copy-start
  7.2 64.4 %all-gather.4.cloned.1.call-start = ((), (), s32[]{:S(2)}) async-start(), calls=%async_computation.2 | async-start | bytes 2621440 | tf_op jit(solution)/shard_map/all_gather | solution.py:39
  9.6 32.1 %copy-start.4 = (s32[64]{0:T(128)S(1)}, s32[64]{0:T(128)}, u32[]{:S(2)}) copy-start(s32[64]{0:T(128)} %param.11) | copy-start | bytes 772
  40.9 66.0 %all-gather.6.cloned.1.call-start = ((), (), s32[]{:S(2)}) async-start(), calls=%async_computation.3 | async-start | bytes 2621440 | tf_op jit(solution)/shard_map/all_gather | solution.py:53
  71.6 35.3 %copy-start.1 = (bf16[1024,1024]{1,0:T(8,128)(2,1)S(1)}, bf16[1024,1024]{1,0:T(8,128)(2,1)}, u32[]{:S(2)}) copy-start(bf16[1024,1024]{1,0:T(8,128)(2,1)} %all-gather.4.cloned.1.call-done) | copy-start | bytes 6291460
  124.5 30.1 %all-to-all-start.1 = ((bf16[64,4,1024]{2,1,0:T(4,128)(2,1)}), bf16[64,4,1024]{2,1,0:T(4,128)(2,1)}, u32[]{:S(2)}, u32[]{:S(2)}) async-start(bf16[64,4,1024]{2,1,0:T(4,128)(2,1)} %all_to_all.27), calls=%async_computation.1 | async-start | bytes 1048576 | tf_op jit(solution)/shard_map/all_to_all | solution.py:60
  137.6 3.1 %copy-start.2 = (bf16[256,1024]{1,0:T(8,128)(2,1)S(1)}, bf16[256,1024]{1,0:T(8,128)(2,1)}, u32[]{:S(2)}) copy-start(bf16[256,1024]{1,0:T(8,128)(2,1)} %all_to_all.26) | copy-start | bytes 1572868
  137.6 3.1 %copy-start.3 = (f32[1,256,1024]{2,1,0:T(8,128)S(1)}, f32[1,256,1024]{2,1,0:T(8,128)}, u32[]{:S(2)}) copy-start(f32[1,256,1024]{2,1,0:T(8,128)} %param.12) | copy-start | bytes 3145732
Sparse Core Ops, SparseCore 0:
  41.0 30.5 all-gather.3
  73.4 33.4 all-gather.5
where the time goes:
time: 168 us; the launch traced here: 167 us
  waiting for transfers between devices  74 us (44%)
  blocking collectives  37.3 us (22%)
  between operations  15.6 us (9%)
  starting transfers between devices  12.9 us (8%)
  other arithmetic  10.6 us (6%)
  matrix products  10.5 us (6%)
  local copies, waits for them, and re-layouts  6.57 us (4%)
    all_gather x1, waiting for transfers between devices, per_device(): lax.all_gather(root_right[0], 'rep', axis=0, tiled=True)  31.2 us
    all_to_all x1, blocking collectives, per_device(): lax.all_to_all(ordered.astype(jnp.bfloat16), 'fsdp', split_axis=1, concat...  30.1 us
    all_gather x1, waiting for transfers between devices, per_device(): lax.all_gather(own_rows.astype(jnp.bfloat16), 'rep', axis=0, tiled=True)  29.9 us
    all_to_all x1, starting transfers between devices, per_device(): lax.all_to_all(direction, 'fsdp', split_axis=0, concat_axis=1, tiled=True)  12.9 us
    all_to_all x1, waiting for transfers between devices, per_device(): lax.all_to_all(direction, 'fsdp', split_axis=0, concat_axis=1, tiled=True)  12.2 us
    psum x1, blocking collectives, per_device(): direction_sq = lax.psum(jnp.sum(precond * precond), 'rep')  7.15 us
    dot_general x1, matrix products, per_device(): jnp.dot(left_prod, lax.all_gather(root_right[0], 'rep', axis=0, tiled=Tru...  5.66 us
    convert_element_type x1, other arithmetic, per_device(): y_new = (0.1 * z_new + 0.9 * x_new).astype(jnp.bfloat16)  3.93 us
  transfers between devices with their start and end apart: 3, of which 3 were waited for; matrix products, arithmetic and copies ran while one was open for 5% of the time, Pallas kernels for 0%

commit v1 on v0

v1 whole, which is shorter than its diff:
```python
import functools

import jax
import jax.numpy as jnp
from jax import lax
from jax.experimental import pallas as pl
from jax.experimental.pallas import tpu as pltpu
from jax.sharding import PartitionSpec as P

MESH = pl.DeviceIdType.MESH
F32 = jnp.float32
BF16 = jnp.bfloat16

NB = 64
BLK = 1024
Q = 256
LINE = 16
CH = 4


def iota(shape, dim):
    return lax.broadcasted_iota(jnp.int32, shape, dim)


def fold(v):
    rows, cols = v.shape
    total = v[:, 0:128]
    for j in range(1, cols // 128):
        total = total + v[:, 128 * j : 128 * (j + 1)]
    return jnp.sum(total.reshape(rows // 8, 8, 128), axis=0)


def remote_kernel(
    inv_ref, own_ref, grad_ref, z_ref, x_ref, sl_ref, sr_ref, rl_ref, rr_ref,
    z_o, x_o, y_o, l_o, r_o,
    gbuf, send, held, gq, bc, ac, lg, lgb, zbuf, xbuf, slbuf, srbuf,
    perm1, perm2, dsend, dret, part, scl, sclsend,
    loc, line_sem, y_s1, y_s2, y_r1, y_r2, g_s, g_r, d_s, d_r, p_s, p_r, s_s, s_r,
):
    f = lax.axis_index("fsdp")
    r = lax.axis_index("rep")
    fx, fz, fc = f // LINE, (f % LINE) // 2, f % 2
    right, left, across = (r + 1) % 4, (r + 3) % 4, (r + 2) % 4

    def peer(j, i):
        return ((fx + j) % 4) * LINE + ((fz + i // 2) % 8) * 2 + (fc + i) % 2

    barrier = pltpu.get_barrier_semaphore()

    def greet(i, c):
        pl.semaphore_signal(barrier, inc=1, device_id={"fsdp": peer(0, i)}, device_id_type=MESH)
        return c

    lax.fori_loop(1, LINE, greet, 0)
    for d in (1, 2, 3):
        pl.semaphore_signal(barrier, inc=1, device_id={"fsdp": peer(d, 0)}, device_id_type=MESH)
        pl.semaphore_signal(barrier, inc=1, device_id={"rep": (r + d) % 4}, device_id_type=MESH)

    loads = [pltpu.make_async_copy(grad_ref, gbuf, loc.at[0])]
    for c in range(CH):
        loads.append(
            pltpu.make_async_copy(rr_ref.at[:, pl.ds(Q * c, Q)], bc.at[c, r], loc.at[1 + c])
        )
    for c in range(4):
        loads.append(
            pltpu.make_async_copy(rl_ref.at[:, pl.ds(Q * c, Q)], ac.at[c], loc.at[5 + c])
        )
    for n, (a, b) in enumerate(((sl_ref, slbuf), (sr_ref, srbuf), (z_ref, zbuf), (x_ref, xbuf))):
        loads.append(pltpu.make_async_copy(a, b, loc.at[9 + n]))
    for load in loads:
        load.start()

    o, i = iota((Q, Q), 0), iota((Q, Q), 1)
    perm1[...] = (((i % 32) // 4) * 32 + (i // 32) * 4 + i % 4 == o).astype(F32).astype(BF16)
    perm2[...] = (((i % 128) // 4) * 8 + (i // 128) * 4 + i % 4 == o).astype(F32).astype(BF16)

    loads[0].wait()

    def prepare(s, c):
        send[s] = gbuf[inv_ref[s]].astype(BF16)
        return c

    lax.fori_loop(0, NB, prepare, 0, unroll=4)
    held[f] = send[f]
    for c in range(CH):
        loads[1 + c].wait()

    def ring(n, ref, sub, half0, half1):
        def first():
            for side, to in ((0, right), (1, left)):
                pltpu.make_async_remote_copy(
                    sub(ref, r), sub(ref, r), y_s1.at[n, side], y_r1.at[n, side],
                    device_id={"rep": to}, device_id_type=MESH,
                ).start()

        def second():
            for side, to, frm, half in ((0, right, left, half0), (1, left, right, half1)):
                pltpu.make_async_remote_copy(
                    sub(ref, frm), sub(ref, frm), y_s1.at[n, side], y_r1.at[n, side],
                    device_id={"rep": to}, device_id_type=MESH,
                ).wait_recv()
                pltpu.make_async_remote_copy(
                    half(ref, frm), half(ref, frm), y_s2.at[n, side], y_r2.at[n, side],
                    device_id={"rep": to}, device_id_type=MESH,
                ).start()

        def done():
            for side, to, half in ((0, right, half0), (1, left, half1)):
                pltpu.make_async_remote_copy(
                    half(ref, across), half(ref, across), y_s2.at[n, side], y_r2.at[n, side],
                    device_id={"rep": to}, device_id_type=MESH,
                ).wait_recv()

        def drain():
            for side, to, half in ((0, right, half0), (1, left, half1)):
                pltpu.make_async_remote_copy(
                    sub(ref, r), sub(ref, r), y_s1.at[n, side], y_r1.at[n, side],
                    device_id={"rep": to}, device_id_type=MESH,
                ).wait_send()
                pltpu.make_async_remote_copy(
                    half(ref, r), half(ref, r), y_s2.at[n, side], y_r2.at[n, side],
                    device_id={"rep": to}, device_id_type=MESH,
                ).wait_send()

        return first, second, done, drain

    def rows_of(start, size):
        return lambda ref, k: ref.at[k, pl.ds(start, size)]

    b_ring = [
        ring(c, bc.at[c], rows_of(0, Q), rows_of(0, Q // 2), rows_of(Q // 2, Q // 2))
        for c in range(CH)
    ]
    g_ring = []
    for j in range(4):
        base = pl.multiple_of(((fx + 4 - j) % 4) * 64, 64)
        g_ring.append(
            ring(4 + j, gq, rows_of(base, 64), rows_of(base, 32), rows_of(base + 32, 32))
        )

    def g_copy(j, i):
        to = peer(j, i)
        return pltpu.make_async_remote_copy(
            send.at[to], held.at[f], g_s.at[0], g_r.at[j],
            device_id={"fsdp": to}, device_id_type=MESH,
        )

    def g_send(j):
        def body(i, c):
            g_copy(j, i).start()
            return c

        lax.fori_loop(1 if j == 0 else 0, LINE, body, 0)

    def g_take(j):
        count = 15 if j == 0 else 16
        pltpu.make_async_remote_copy(
            send.at[pl.ds(0, count)], held.at[pl.ds(0, count)], g_s.at[0], g_r.at[j],
            device_id={"fsdp": peer(1, 0)}, device_id_type=MESH,
        ).wait_recv()
        line = (fx + 4 - j) % 4
        pieces = jnp.concatenate(
            [held[pl.ds(line * LINE + 8 * h, 8)].reshape(Q, 128) for h in range(2)], axis=1
        )
        rows = jnp.dot(perm1[...], pieces, preferred_element_type=F32).astype(BF16)
        for h in range(2):
            at = pl.multiple_of(line * 64 + 32 * h, 32)
            for t in range(8):
                gq[r, pl.ds(at, 32), 128 * t : 128 * (t + 1)] = rows[
                    32 * t : 32 * (t + 1), 128 * h : 128 * (h + 1)
                ]

    pl.semaphore_wait(barrier, 21)
    for d in (1, 2, 3):
        pl.semaphore_signal(line_sem, inc=1, device_id={"fsdp": peer(d, 0)}, device_id_type=MESH)
    g_send(0)
    b_ring[0][0]()
    b_ring[1][0]()
    pl.semaphore_wait(line_sem, 3)
    for j in range(1, 4):
        g_send(j)

    for load in loads[5:]:
        load.wait()

    def left_root(k, first):
        gk = gq.at[k]
        for n in range(4):
            cols = slice(Q * n, Q * (n + 1))
            term = jnp.dot(ac[k], gk[:, cols], preferred_element_type=F32)
            lg[:, cols] = term if first else lg[:, cols] + term

    def stats(k, first):
        gk = gq.at[k]
        l_o[:, pl.ds(pl.multiple_of(k * Q, Q), Q)] = lax.dot_general(
            gq[r], gk[...], (((1,), (1,)), ((), ())), preferred_element_type=F32
        )
        strip = gk[:, pl.ds(pl.multiple_of(r * Q, Q), Q)]
        for n in range(4):
            cols = slice(Q * n, Q * (n + 1))
            term = lax.dot_general(
                strip, gk[:, cols], (((0,), (0,)), ((), ())), preferred_element_type=F32
            )
            r_o[:, cols] = term if first else r_o[:, cols] + term

    b_ring[0][1]()
    g_take(0)
    g_ring[0][0]()
    b_ring[1][1]()
    g_take(1)
    g_ring[1][0]()
    g_ring[0][1]()
    g_take(2)
    g_ring[2][0]()
    g_ring[1][1]()
    g_take(3)
    g_ring[3][0]()
    b_ring[2][0]()
    own = gq[r].astype(F32)
    part[r, 1] = fold(own * own)
    left_root(r, True)
    stats(r, True)
    g_ring[2][1]()
    g_ring[3][1]()
    b_ring[3][0]()
    left_root(left, False)
    left_root(right, False)
    b_ring[2][1]()
    stats(left, False)
    for n in range(4):
        g_ring[n][2]()
    left_root(across, False)
    lgb[...] = lg[...].astype(BF16)

    def d_send(c):
        def body(i, carry):
            to = peer(i // LINE, i % LINE)
            pltpu.make_async_remote_copy(
                dsend.at[c, to], dret.at[c, f], d_s.at[c], d_r.at[c],
                device_id={"fsdp": to}, device_id_type=MESH,
            ).start()
            return carry

        lax.fori_loop(1, NB, body, 0)
        dret[c, f] = dsend[c, f]

    def product(c):
        b_ring[c][2]()
        p = jnp.dot(lgb[...], bc[c].reshape(BLK, Q), preferred_element_type=F32)
        squares = fold(p * p)
        part[r, 0] = squares if c == 0 else part[r, 0] + squares
        pb = p.astype(BF16)
        for h in range(2):
            rows = slice(128 * h, 128 * (h + 1))
            pieces = jnp.concatenate([pb[rows, 0:128], pb[rows, 128:256]], axis=0)
            out = jnp.dot(perm2[...], pieces, preferred_element_type=F32)
            dsend[c, 32 * h : 32 * (h + 1)] = out.reshape(32, 8, 128).astype(BF16)
        d_send(c)

    product(0)
    product(1)
    b_ring[3][1]()
    product(2)
    product(3)

    def p_copy(d):
        return pltpu.make_async_remote_copy(
            part.at[r], part.at[r], p_s.at[d - 1], p_r.at[d - 1],
            device_id={"rep": (r + d) % 4}, device_id_type=MESH,
        )

    for d in (1, 2, 3):
        p_copy(d).start()
    stats(right, False)
    stats(across, False)
    for d in (1, 2, 3):
        p_copy(d).wait_recv()
    entries = float(BLK * BLK)
    sums = part[0] + part[1] + part[2] + part[3]
    d_sq = jnp.sum(jnp.sum(sums[0], axis=0, keepdims=True), axis=1, keepdims=True)
    g_sq = jnp.sum(jnp.sum(sums[1], axis=0, keepdims=True), axis=1, keepdims=True)
    scale = jnp.sqrt(g_sq / entries) * lax.rsqrt(d_sq / entries + 1e-06)
    row = jnp.broadcast_to(scale, (1, 128))
    sclsend[...] = row
    scl[f] = row

    def s_copy(i):
        return pltpu.make_async_remote_copy(
            sclsend, scl.at[f], s_s.at[0], s_r.at[0],
            device_id={"fsdp": peer(i // LINE, i % LINE)}, device_id_type=MESH,
        )

    def s_start(i, carry):
        s_copy(i).start()
        return carry

    lax.fori_loop(1, NB, s_start, 0)
    l_o[...] = 0.95 * slbuf[...] + (0.05 / BLK) * l_o[...]
    r_o[...] = 0.95 * srbuf[...] + (0.05 / BLK) * r_o[...]

    for c in range(CH):
        pltpu.make_async_remote_copy(
            dsend.at[c, pl.ds(0, NB - 1)], dret.at[c, pl.ds(0, NB - 1)], d_s.at[c], d_r.at[c],
            device_id={"fsdp": peer(1, 0)}, device_id_type=MESH,
        ).wait()
    scales = pltpu.make_async_remote_copy(
        scl.at[pl.ds(0, NB - 1)], scl.at[pl.ds(0, NB - 1)], s_s.at[0], s_r.at[0],
        device_id={"fsdp": peer(1, 0)}, device_id_type=MESH,
    )
    scales.wait()

    def update(b, carry):
        s = own_ref[b]
        step = 0.2 * scl[s]
        d = jnp.concatenate([dret[c, s].astype(F32) for c in range(CH)], axis=0)
        z = zbuf[b] - step * d
        x = 0.75 * xbuf[b] + 0.25 * z
        z_o[b] = z
        x_o[b] = x
        y_o[b] = (0.1 * z + 0.9 * x).astype(BF16)
        return carry

    lax.fori_loop(0, NB, update, 0, unroll=4)

    pltpu.make_async_remote_copy(
        send.at[pl.ds(0, NB - 1)], held.at[pl.ds(0, NB - 1)], g_s.at[0], g_r.at[0],
        device_id={"fsdp": peer(1, 0)}, device_id_type=MESH,
    ).wait_send()
    for n in range(4):
        b_ring[n][3]()
        g_ring[n][3]()
    for d in (1, 2, 3):
        p_copy(d).wait_send()


def write_kernel(z, x, y, l, r, z_o, x_o, y_o, l_o, r_o, sem):
    copies = [
        pltpu.make_async_copy(a, b, sem.at[n])
        for n, (a, b) in enumerate(((z, z_o), (x, x_o), (y, y_o), (l, l_o), (r, r_o)))
    ]
    for copy in copies:
        copy.start()
    for copy in copies:
        copy.wait()


def pieces_of(flat):
    return flat[0].reshape(4, 512, 128).transpose(1, 0, 2).reshape(NB, 32, 128)


def flat_of(pieces):
    return pieces.reshape(512, 4, 128).transpose(1, 0, 2).reshape(1, 4, 65536)


def per_device(grad, z_params, x_params, owner, stat_left, stat_right, root_left, root_right):
    slots = jnp.arange(NB, dtype=jnp.int32)
    inverse = jnp.sum(jnp.where(owner[None, :] == slots[:, None], slots[None, :], 0), axis=1)
    smem = pl.BlockSpec(memory_space=pltpu.SMEM)
    hbm = pl.BlockSpec(memory_space=pltpu.HBM)
    vmem = pl.BlockSpec(memory_space=pltpu.VMEM)
    anywhere = pl.BlockSpec(memory_space=pl.ANY)
    shapes = (
        ((NB, 32, 128), F32),
        ((NB, 32, 128), F32),
        ((NB, 32, 128), BF16),
        ((Q, BLK), F32),
        ((Q, BLK), F32),
    )
    dma = pltpu.SemaphoreType.DMA
    results = pl.pallas_call(
        remote_kernel,
        out_shape=tuple(pltpu.VMEM(s, t) for s, t in shapes),
        in_specs=[smem, smem] + [hbm] * 7,
        out_specs=(vmem,) * 5,
        scratch_shapes=[
            pltpu.VMEM((NB, 32, 128), F32),
            pltpu.VMEM((NB, 32, 128), BF16),
            pltpu.VMEM((NB, 32, 128), BF16),
            pltpu.VMEM((4, Q, BLK), BF16),
            pltpu.VMEM((CH, 4, Q, Q), BF16),
            pltpu.VMEM((4, Q, Q), BF16),
            pltpu.VMEM((Q, BLK), F32),
            pltpu.VMEM((Q, BLK), BF16),
            pltpu.VMEM((NB, 32, 128), F32),
            pltpu.VMEM((NB, 32, 128), F32),
            pltpu.VMEM((Q, BLK), F32),
            pltpu.VMEM((Q, BLK), F32),
            pltpu.VMEM((Q, Q), BF16),
            pltpu.VMEM((Q, Q), BF16),
            pltpu.VMEM((CH, NB, 8, 128), BF16),
            pltpu.VMEM((CH, NB, 8, 128), BF16),
            pltpu.VMEM((4, 2, 8, 128), F32),
            pltpu.VMEM((NB, 1, 128), F32),
            pltpu.VMEM((1, 128), F32),
            dma((13,)),
            pltpu.SemaphoreType.REGULAR,
            dma((8, 2)),
            dma((8, 2)),
            dma((8, 2)),
            dma((8, 2)),
            dma((1,)),
            dma((4,)),
            dma((CH,)),
            dma((CH,)),
            dma((3,)),
            dma((3,)),
            dma((1,)),
            dma((1,)),
        ],
        compiler_params=pltpu.CompilerParams(
            collective_id=0, has_side_effects=True, vmem_limit_bytes=36 << 20
        ),
        name="shampoo",
    )(
        inverse, owner, pieces_of(grad), pieces_of(z_params), pieces_of(x_params),
        stat_left[0], stat_right[0], root_left[0], root_right[0],
    )
    z, x, y, left_new, right_new = pl.pallas_call(
        write_kernel,
        out_shape=tuple(jax.ShapeDtypeStruct(s, t) for s, t in shapes),
        in_specs=[vmem] * 5,
        out_specs=(anywhere,) * 5,
        scratch_shapes=[dma((5,))],
        compiler_params=pltpu.CompilerParams(vmem_limit_bytes=8 << 20),
        name="write",
    )(*results)
    return (flat_of(z), flat_of(x), flat_of(y), left_new[None], right_new[None])


def solution(mesh):
    return jax.shard_map(
        per_device,
        mesh=mesh,
        in_specs=(P("rep", "fsdp", None),) * 3 + (P(),) + (P("fsdp", "rep", None),) * 4,
        out_specs=(P("rep", "fsdp", None),) * 3 + (P("fsdp", "rep", None),) * 2,
        check_vma=False,
    )
```

time: 168 us -> 78.4 us (0.47)
  waiting for transfers between devices: 74 us -> 0 us
  Pallas kernels: 0 us -> 68.4 us
  blocking collectives: 37.3 us -> 0 us
  between operations: 15.6 us -> 0.66 us
  starting transfers between devices: 12.9 us -> 0 us
  matrix products: 10.5 us -> 0 us
  other arithmetic: 10.6 us -> 0.11 us
  local copies, waits for them, and re-layouts: 6.57 us -> 8.85 us
    pallas_call x0 -> x2, Pallas kernels: none -> 68.4 us  [the longest x1 66.1 us: per_device(): pl.pallas_call(remote_kernel, out_shape=tuple((pltpu.VMEM(s, t) for s, t...]
    all_gather x2 -> x0, waiting for transfers between devices: 61.1 us -> none  [the longest x1 31.2 us: per_device(): lax.all_gather(root_right[0], 'rep', axis=0, tiled=True)]
    all_to_all x1 -> x0, blocking collectives: 30.1 us -> none  [per_device(): lax.all_to_all(ordered.astype(jnp.bfloat16), 'fsdp', split_axis=1, concat...]
    all_to_all x1 -> x0, starting transfers between devices: 12.9 us -> none  [per_device(): lax.all_to_all(direction, 'fsdp', split_axis=0, concat_axis=1, tiled=True)]
    all_to_all x1 -> x0, waiting for transfers between devices: 12.2 us -> none  [per_device(): lax.all_to_all(direction, 'fsdp', split_axis=0, concat_axis=1, tiled=True)]
    dot_general x3 -> x0, matrix products: 10.5 us -> none  [the longest x1 5.66 us: per_device(): jnp.dot(left_prod, lax.all_gather(root_right[0], 'rep', axis=0, tiled=Tru...]
    unnamed x12 -> x16, local copies, waits for them, and re-layouts: 0.45 us -> 8.85 us
    psum x1 -> x0, blocking collectives: 7.15 us -> none  [per_device(): direction_sq = lax.psum(jnp.sum(precond * precond), 'rep')]
  transfers between devices with their start and end apart: 3 -> 0, of which waited for: 3 -> 0; matrix products, arithmetic and copies ran while one was open for 5% -> 0% of each run, Pallas kernels for 0% -> 0%
where the time goes in v1:
time: 78.4 us; the launch traced here: 78 us
  Pallas kernels  68.4 us (87%)
  local copies, waits for them, and re-layouts  8.85 us (11%)
    pallas_call x1, Pallas kernels, per_device(): pl.pallas_call(remote_kernel, out_shape=tuple((pltpu.VMEM(s, t) for s, t...  66.1 us
    unnamed x16, local copies, waits for them, and re-layouts  8.85 us
    pallas_call x1, Pallas kernels, per_device(): pl.pallas_call(write_kernel, out_shape=tuple((jax.ShapeDtypeStruct(s, t)...  2.22 us

profile of v1, /device:TPU:1, one launch (start us, length us, event | category | flops | bytes accessed | tf_op | source)
XLA Modules:
  0.0 78.0 jit_solution(674323685468601671)
XLA Ops:
  0.6 0.0 copy-start.7
  0.6 0.6 copy-done.7
  1.3 0.1 select_reduce_fusion.inv_ref
  1.4 0.0 copy-start
  1.4 1.2 %copy-done = f32[1,4,65536]{2,1,0:T(4,128)S(1)} copy-done((f32[1,4,65536]{2,1,0:T(4,128)S(1)}, f32[1,4,65536]{2,1,0:T(4,128)}, u32[]{:S(2)}) %copy-start) | copy-done | bytes 1048600
  2.6 0.0 copy-start.1
  2.6 1.2 %copy-done.1 = f32[1,4,65536]{2,1,0:T(4,128)S(1)} copy-done((f32[1,4,65536]{2,1,0:T(4,128)S(1)}, f32[1,4,65536]{2,1,0:T(4,128)}, u32[]{:S(2)}) %copy-start.1) | copy-done | bytes 1048600
  3.9 0.0 copy-start.2
  3.9 1.2 %copy-done.2 = f32[1,4,65536]{2,1,0:T(4,128)S(1)} copy-done((f32[1,4,65536]{2,1,0:T(4,128)S(1)}, f32[1,4,65536]{2,1,0:T(4,128)}, u32[]{:S(2)}) %copy-start.2) | copy-done | bytes 1048600
  5.1 0.0 copy-start.3
  5.1 1.2 %copy-done.3 = f32[1,256,1024]{2,1,0:T(8,128)S(1)} copy-done((f32[1,256,1024]{2,1,0:T(8,128)S(1)}, f32[1,256,1024]{2,1,0:T(8,128)}, u32[]{:S(2)}) %copy-start.3) | copy-done | bytes 1048600
  6.3 0.0 copy-start.4
  6.3 1.2 %copy-done.4 = f32[1,256,1024]{2,1,0:T(8,128)S(1)} copy-done((f32[1,256,1024]{2,1,0:T(8,128)S(1)}, f32[1,256,1024]{2,1,0:T(8,128)}, u32[]{:S(2)}) %copy-start.4) | copy-done | bytes 1048600
  7.5 0.0 copy-start.5
  7.5 1.0 %copy-done.5 = bf16[1,256,1024]{2,1,0:T(8,128)(2,1)S(1)} copy-done((bf16[1,256,1024]{2,1,0:T(8,128)(2,1)S(1)}, bf16[1,256,1024]{2,1,0:T(8,128)(2,1)}, u32[]{:S(2)}) %copy-start.5) | copy-done | bytes 524312
  8.6 0.0 copy-start.6
  8.6 1.0 %copy-done.6 = bf16[1,256,1024]{2,1,0:T(8,128)(2,1)S(1)} copy-done((bf16[1,256,1024]{2,1,0:T(8,128)(2,1)S(1)}, bf16[1,256,1024]{2,1,0:T(8,128)(2,1)}, u32[]{:S(2)}) %copy-start.6) | copy-done | bytes 524312
  9.6 66.1 %shampoo.1 = (f32[64,32,128]{2,1,0:T(8,128)S(1)}, f32[64,32,128]{2,1,0:T(8,128)S(1)}, bf16[64,32,128]{2,1,0:T(8,128)(2,1)S(1)}, f32[256,1024]{1,0:T(8,128)S(1)}, f32[256,1024]{1,0:T(8,128)S(1)}) custom-call(s32[64]{0:T(128)S(1)} %select_reduce_fusion.inv_ref, s32[64]{0:T(128)S(1)} %copy-done.7, f32[64,32,128]{2,1,0:T(8,128)S(1)} %bitcast.36, ...), custom_call_target="tpu_custom_call" | custom-call | tf_op jit(solution)/shard_map/shampoo/pallas_call | solution.py:370
  75.8 2.2 %write.1 = (f32[64,32,128]{2,1,0:T(8,128)}, f32[64,32,128]{2,1,0:T(8,128)}, bf16[64,32,128]{2,1,0:T(8,128)(2,1)}, f32[256,1024]{1,0:T(8,128)}, f32[256,1024]{1,0:T(8,128)}) custom-call(f32[64,32,128]{2,1,0:T(8,128)S(1)} %get-tuple-element.15.z, f32[64,32,128]{2,1,0:T(8,128)S(1)} %get-tuple-element.16.x, bf16[64,32,128]{2,1,0:T(8,128)(2,1)S(1)} %get-tuple-element.17.y, ...), custom_call_target="tpu_custom_call" | custom-call | tf_op jit(solution)/shard_map/write/pallas_call | solution.py:418
Async XLA Ops:
  0.6 0.7 copy-start.7
  1.4 1.2 %copy-start = (f32[1,4,65536]{2,1,0:T(4,128)S(1)}, f32[1,4,65536]{2,1,0:T(4,128)}, u32[]{:S(2)}) copy-start(f32[1,4,65536]{2,1,0:T(4,128)} %param.8) | copy-start | bytes 3145732
  2.6 1.2 %copy-start.1 = (f32[1,4,65536]{2,1,0:T(4,128)S(1)}, f32[1,4,65536]{2,1,0:T(4,128)}, u32[]{:S(2)}) copy-start(f32[1,4,65536]{2,1,0:T(4,128)} %param.9) | copy-start | bytes 3145732
  3.9 1.2 %copy-start.2 = (f32[1,4,65536]{2,1,0:T(4,128)S(1)}, f32[1,4,65536]{2,1,0:T(4,128)}, u32[]{:S(2)}) copy-start(f32[1,4,65536]{2,1,0:T(4,128)} %param.10) | copy-start | bytes 3145732
  5.1 1.2 %copy-start.3 = (f32[1,256,1024]{2,1,0:T(8,128)S(1)}, f32[1,256,1024]{2,1,0:T(8,128)}, u32[]{:S(2)}) copy-start(f32[1,256,1024]{2,1,0:T(8,128)} %param.12) | copy-start | bytes 3145732
  6.3 1.2 %copy-start.4 = (f32[1,256,1024]{2,1,0:T(8,128)S(1)}, f32[1,256,1024]{2,1,0:T(8,128)}, u32[]{:S(2)}) copy-start(f32[1,256,1024]{2,1,0:T(8,128)} %param.13) | copy-start | bytes 3145732
  7.5 1.0 %copy-start.5 = (bf16[1,256,1024]{2,1,0:T(8,128)(2,1)S(1)}, bf16[1,256,1024]{2,1,0:T(8,128)(2,1)}, u32[]{:S(2)}) copy-start(bf16[1,256,1024]{2,1,0:T(8,128)(2,1)} %param.14) | copy-start | bytes 1572868
  8.6 1.0 %copy-start.6 = (bf16[1,256,1024]{2,1,0:T(8,128)(2,1)S(1)}, bf16[1,256,1024]{2,1,0:T(8,128)(2,1)}, u32[]{:S(2)}) copy-start(bf16[1,256,1024]{2,1,0:T(8,128)(2,1)} %param.15) | copy-start | bytes 1572868

commit v2 on v1

--- a/solution.py
+++ b/solution.py
@@ -356,7 +356,6 @@
     slots = jnp.arange(NB, dtype=jnp.int32)
     inverse = jnp.sum(jnp.where(owner[None, :] == slots[:, None], slots[None, :], 0), axis=1)
     smem = pl.BlockSpec(memory_space=pltpu.SMEM)
-    hbm = pl.BlockSpec(memory_space=pltpu.HBM)
     vmem = pl.BlockSpec(memory_space=pltpu.VMEM)
     anywhere = pl.BlockSpec(memory_space=pl.ANY)
     shapes = (
@@ -370,7 +369,7 @@
     results = pl.pallas_call(
         remote_kernel,
         out_shape=tuple(pltpu.VMEM(s, t) for s, t in shapes),
-        in_specs=[smem, smem] + [hbm] * 7,
+        in_specs=[smem, smem] + [anywhere] * 7,
         out_specs=(vmem,) * 5,
         scratch_shapes=[
             pltpu.VMEM((NB, 32, 128), F32),
@@ -408,7 +407,7 @@
             dma((1,)),
         ],
         compiler_params=pltpu.CompilerParams(
-            collective_id=0, has_side_effects=True, vmem_limit_bytes=36 << 20
+            collective_id=0, has_side_effects=True, vmem_limit_bytes=57 << 20
         ),
         name="shampoo",
     )(

time: 78.4 us -> 70.5 us (0.90)
  local copies, waits for them, and re-layouts: 8.85 us -> 0.65 us
    unnamed x16 -> x2, local copies, waits for them, and re-layouts: 8.85 us -> 0.65 us
where the time goes in v2:
time: 70.5 us; the launch traced here: 70.4 us
  Pallas kernels  68.5 us (97%)
    pallas_call x1, Pallas kernels, per_device(): pl.pallas_call(remote_kernel, out_shape=tuple((pltpu.VMEM(s, t) for s, t...  66.3 us
    pallas_call x1, Pallas kernels, per_device(): pl.pallas_call(write_kernel, out_shape=tuple((jax.ShapeDtypeStruct(s, t)...  2.22 us

profile of v2, /device:TPU:1, one launch (start us, length us, event | category | flops | bytes accessed | tf_op | source)
XLA Modules:
  0.0 70.4 jit_solution(9417444522575065367)
XLA Ops:
  0.6 0.0 copy-start
  0.6 0.6 copy-done
  1.3 0.6 select_reduce_fusion.inv_ref
  1.9 66.3 %shampoo.1 = (f32[64,32,128]{2,1,0:T(8,128)S(1)}, f32[64,32,128]{2,1,0:T(8,128)S(1)}, bf16[64,32,128]{2,1,0:T(8,128)(2,1)S(1)}, f32[256,1024]{1,0:T(8,128)S(1)}, f32[256,1024]{1,0:T(8,128)S(1)}) custom-call(s32[64]{0:T(128)} %select_reduce_fusion.inv_ref, s32[64]{0:T(128)} %own_ref.1, f32[64,32,128]{2,1,0:T(8,128)} %bitcast.36, f32[64,32,128]{2,1,0:T(8,128)} %bitcast.37, ...), custom_call_target="tpu_custom_call" | custom-call | tf_op jit(solution)/shard_map/shampoo/pallas_call | solution.py:369
  68.2 2.2 %write.1 = (f32[64,32,128]{2,1,0:T(8,128)}, f32[64,32,128]{2,1,0:T(8,128)}, bf16[64,32,128]{2,1,0:T(8,128)(2,1)}, f32[256,1024]{1,0:T(8,128)}, f32[256,1024]{1,0:T(8,128)}) custom-call(f32[64,32,128]{2,1,0:T(8,128)S(1)} %get-tuple-element.15.z, f32[64,32,128]{2,1,0:T(8,128)S(1)} %get-tuple-element.16.x, bf16[64,32,128]{2,1,0:T(8,128)(2,1)S(1)} %get-tuple-element.17.y, ...), custom_call_target="tpu_custom_call" | custom-call | tf_op jit(solution)/shard_map/write/pallas_call | solution.py:417
Async XLA Ops:
  0.6 0.7 copy-start

commit v3 on v2

v3 whole, which is shorter than its diff:
```python
import functools

import jax
import jax.numpy as jnp
from jax import lax
from jax.experimental import pallas as pl
from jax.experimental.pallas import tpu as pltpu
from jax.sharding import PartitionSpec as P

MESH = pl.DeviceIdType.MESH
F32 = jnp.float32
BF16 = jnp.bfloat16

NB = 64
BLK = 1024
Q = 256
LINE = 16
GC = 8
CH = 4


def iota(shape, dim):
    return lax.broadcasted_iota(jnp.int32, shape, dim)


def fold(v):
    rows, cols = v.shape
    total = v[:, 0:128]
    for j in range(1, cols // 128):
        total = total + v[:, 128 * j : 128 * (j + 1)]
    return jnp.sum(total.reshape(rows // 8, 8, 128), axis=0)


def remote_kernel(
    own_ref, grad_ref, z_ref, x_ref, sl_ref, sr_ref, rl_ref, rr_ref,
    z_o, x_o, y_o, l_o, r_o,
    gbuf, send, held, gq, bc, ac, lg, lgb, zbuf, xbuf, slbuf, srbuf,
    perm1, perm2, dsend, dret, part, scl, sclsend, spread, invv, inv,
    loc, line_sem, core_sem, y_s1, y_s2, y_r1, y_r2, g_s, g_r, d_s, d_r, p_s, p_r, s_s, s_r,
):
    f = lax.axis_index("fsdp")
    r = lax.axis_index("rep")
    fx, fz, fc = f // LINE, (f % LINE) // 2, f % 2
    other = f + 1 - 2 * fc
    right, left, across = (r + 1) % 4, (r + 3) % 4, (r + 2) % 4

    def peer(j, h, i):
        z = ((fz // 4 + h) % 2) * 4 + (fz + i // 2) % 4
        return ((fx + j) % 4) * LINE + z * 2 + (fc + i) % 2

    def peer_of(n):
        return peer(n // LINE, (n // 8) % 2, n % 8)

    barrier = pltpu.get_barrier_semaphore()

    def greet(to):
        pl.semaphore_signal(barrier, inc=1, device_id=to, device_id_type=MESH)

    greet({"fsdp": other, "rep": r})
    for d in (1, 2, 3):
        greet({"fsdp": f - fc, "rep": (r + d) % 4})
    for d in range(1, 8):
        greet({"fsdp": fx * LINE + ((fz + d) % 8) * 2 + 1, "rep": r})
    for d in (1, 2, 3):
        greet({"fsdp": ((fx + d) % 4) * LINE + fz * 2 + 1, "rep": r})

    loads = []
    for c in range(CH):
        loads.append(
            pltpu.make_async_copy(rr_ref.at[:, pl.ds(Q * c, Q)], bc.at[c, r], loc.at[1 + c])
        )
    loads.append(pltpu.make_async_copy(grad_ref, gbuf, loc.at[0]))
    for c in range(4):
        loads.append(
            pltpu.make_async_copy(rl_ref.at[:, pl.ds(Q * c, Q)], ac.at[c], loc.at[5 + c])
        )
    for n, (a, b) in enumerate(((sl_ref, slbuf), (sr_ref, srbuf), (z_ref, zbuf), (x_ref, xbuf))):
        loads.append(pltpu.make_async_copy(a, b, loc.at[9 + n]))
    for load in loads:
        load.start()

    def spread_row(b, c):
        spread[pl.ds(b, 1), :] = jnp.full((1, 128), own_ref[b], jnp.int32)
        return c

    lax.fori_loop(0, NB, spread_row, 0, unroll=8)
    hits = jnp.where(spread[...] == iota((NB, 128), 1), iota((NB, 128), 0), 0)
    invv[...] = jnp.max(hits, axis=0, keepdims=True)
    to_smem = pltpu.make_async_copy(invv, inv, loc.at[13])
    to_smem.start()

    def ring(n, ref, sub, half0, half1):
        def copy(part_of, k, side, to, s_sem, r_sem):
            return pltpu.make_async_remote_copy(
                part_of(ref, k), part_of(ref, k), s_sem.at[n, side], r_sem.at[n, side],
                device_id={"rep": to}, device_id_type=MESH,
            )

        def first():
            for side, to in ((0, right), (1, left)):
                copy(sub, r, side, to, y_s1, y_r1).start()

        def second():
            for side, to, frm, half in ((0, right, left, half0), (1, left, right, half1)):
                copy(sub, frm, side, to, y_s1, y_r1).wait_recv()
                copy(half, frm, side, to, y_s2, y_r2).start()

        def done():
            for side, to, half in ((0, right, half0), (1, left, half1)):
                copy(half, across, side, to, y_s2, y_r2).wait_recv()

        def drain():
            for side, to, half in ((0, right, half0), (1, left, half1)):
                copy(sub, r, side, to, y_s1, y_r1).wait_send()
                copy(half, r, side, to, y_s2, y_r2).wait_send()

        return first, second, done, drain

    def rows_of(start, size):
        return lambda ref, k: ref.at[k, pl.ds(start, size)]

    b_ring = [
        ring(c, bc.at[c], rows_of(0, Q), rows_of(0, Q // 2), rows_of(Q // 2, Q // 2))
        for c in range(CH)
    ]

    def place(q):
        return ((fx + 4 - q // 2) % 4) * LINE + ((fz // 4 + q) % 2) * 8

    g_ring = []
    for q in range(GC):
        base = pl.multiple_of(place(q) * 4, 32)
        g_ring.append(
            ring(CH + q, gq, rows_of(base, 32), rows_of(base, 16), rows_of(base + 16, 16))
        )

    for c in range(CH):
        loads[c].wait()

    @pl.when(fc == 0)
    def _():
        pl.semaphore_wait(barrier, 7)
        pl.semaphore_signal(
            core_sem, inc=1, device_id={"fsdp": other, "rep": r}, device_id_type=MESH
        )

    @pl.when(fc == 1)
    def _():
        pl.semaphore_wait(core_sem, 1)

    for c in range(2):
        b_ring[c][0]()

    o, i = iota((Q, Q), 0), iota((Q, Q), 1)
    perm1[...] = (((i % 32) // 4) * 32 + (i // 32) * 4 + i % 4 == o).astype(F32).astype(BF16)
    perm2[...] = (((i % 128) // 4) * 8 + (i // 128) * 4 + i % 4 == o).astype(F32).astype(BF16)

    to_smem.wait()
    loads[4].wait()

    def prepare(s, c):
        send[s] = gbuf[inv[0, s]].astype(BF16)
        return c

    lax.fori_loop(0, NB, prepare, 0, unroll=8)
    held[f] = send[f]

    def g_send(q):
        def body(n, c):
            to = peer_of(n)
            pltpu.make_async_remote_copy(
                send.at[to], held.at[f], g_s.at[0], g_r.at[q],
                device_id={"fsdp": to}, device_id_type=MESH,
            ).start()
            return c

        lax.fori_loop(1 if q == 0 else 8 * q, 8 * q + 8, body, 0)

    def g_take(q):
        count = 7 if q == 0 else 8
        pltpu.make_async_remote_copy(
            send.at[pl.ds(0, count)], held.at[pl.ds(0, count)], g_s.at[0], g_r.at[q],
            device_id={"fsdp": other}, device_id_type=MESH,
        ).wait_recv()
        at = place(q)
        pieces = held[pl.ds(at, 8)].reshape(Q, 128)
        rows = jnp.dot(perm1[...], pieces, preferred_element_type=F32).astype(BF16)
        base = pl.multiple_of(at * 4, 32)
        for t in range(8):
            gq[r, pl.ds(base, 32), 128 * t : 128 * (t + 1)] = rows[32 * t : 32 * (t + 1)]

    @pl.when(fc == 1)
    def _():
        pl.semaphore_wait(barrier, 21)
        pl.semaphore_signal(
            core_sem, inc=1, device_id={"fsdp": other, "rep": r}, device_id_type=MESH
        )

    @pl.when(fc == 0)
    def _():
        pl.semaphore_wait(core_sem, 1)

    for d in (1, 2, 3):
        pl.semaphore_signal(
            line_sem, inc=1, device_id={"fsdp": peer(d, 0, 0)}, device_id_type=MESH
        )
    g_send(0)
    g_send(1)
    pl.semaphore_wait(line_sem, 3)
    for q in range(2, GC):
        g_send(q)

    for load in loads[5:]:
        load.wait()

    def left_root(k, first):
        gk = gq.at[k]
        for n in range(4):
            cols = slice(Q * n, Q * (n + 1))
            term = jnp.dot(ac[k], gk[:, cols], preferred_element_type=F32)
            lg[:, cols] = term if first else lg[:, cols] + term

    def stats(k, first):
        gk = gq.at[k]
        l_o[:, pl.ds(pl.multiple_of(k * Q, Q), Q)] = lax.dot_general(
            gq[r], gk[...], (((1,), (1,)), ((), ())), preferred_element_type=F32
        )
        strip = gk[:, pl.ds(pl.multiple_of(r * Q, Q), Q)]
        for n in range(4):
            cols = slice(Q * n, Q * (n + 1))
            term = lax.dot_general(
                strip, gk[:, cols], (((0,), (0,)), ((), ())), preferred_element_type=F32
            )
            r_o[:, cols] = term if first else r_o[:, cols] + term

    b_ring[0][1]()
    b_ring[1][1]()
    for q in range(GC):
        g_take(q)
        g_ring[q][0]()
        if q >= 2:
            g_ring[q - 2][1]()
    g_ring[GC - 2][1]()
    left_root(r, True)
    g_ring[GC - 1][1]()
    b_ring[2][0]()
    b_ring[3][0]()
    left_root(left, False)
    left_root(right, False)
    own = gq[r].astype(F32)
    part[r, 1] = fold(own * own)
    for q in range(GC):
        g_ring[q][2]()
    left_root(across, False)
    lgb[...] = lg[...].astype(BF16)

    def p_copy(d):
        return pltpu.make_async_remote_copy(
            part.at[r], part.at[r], p_s.at[d - 1], p_r.at[d - 1],
            device_id={"rep": (r + d) % 4}, device_id_type=MESH,
        )

    def product(c):
        b_ring[c][2]()
        p = jnp.dot(lgb[...], bc[c].reshape(BLK, Q), preferred_element_type=F32)
        squares = fold(p * p)
        part[r, 0] = squares if c == 0 else part[r, 0] + squares
        if c == CH - 1:
            for d in (1, 2, 3):
                p_copy(d).start()
        pb = p.astype(BF16)
        for h in range(2):
            rows = slice(128 * h, 128 * (h + 1))
            pieces = jnp.concatenate([pb[rows, 0:128], pb[rows, 128:256]], axis=0)
            out = jnp.dot(perm2[...], pieces, preferred_element_type=F32)
            dsend[c // 2, 32 * h : 32 * (h + 1), c % 2] = out.reshape(32, 8, 128).astype(BF16)

    def d_send(p):
        def body(n, carry):
            to = peer_of(n)
            pltpu.make_async_remote_copy(
                dsend.at[p, to], dret.at[p, f], d_s.at[p], d_r.at[p],
                device_id={"fsdp": to}, device_id_type=MESH,
            ).start()
            return carry

        lax.fori_loop(1, NB, body, 0)
        dret[p, f] = dsend[p, f]

    product(0)
    product(1)
    d_send(0)
    b_ring[2][1]()
    stats(r, True)
    b_ring[3][1]()
    product(2)
    product(3)
    d_send(1)
    stats(left, False)
    stats(right, False)
    for d in (1, 2, 3):
        p_copy(d).wait_recv()
    entries = float(BLK * BLK)
    sums = part[0] + part[1] + part[2] + part[3]
    d_sq = jnp.sum(jnp.sum(sums[0], axis=0, keepdims=True), axis=1, keepdims=True)
    g_sq = jnp.sum(jnp.sum(sums[1], axis=0, keepdims=True), axis=1, keepdims=True)
    scale = jnp.sqrt(g_sq / entries) * lax.rsqrt(d_sq / entries + 1e-06)
    row = jnp.broadcast_to(scale, (1, 128))
    sclsend[...] = row
    scl[f] = row

    def s_start(n, carry):
        pltpu.make_async_remote_copy(
            sclsend, scl.at[f], s_s.at[0], s_r.at[0],
            device_id={"fsdp": peer_of(n)}, device_id_type=MESH,
        ).start()
        return carry

    lax.fori_loop(1, NB, s_start, 0)
    stats(across, False)
    l_o[...] = 0.95 * slbuf[...] + (0.05 / BLK) * l_o[...]
    r_o[...] = 0.95 * srbuf[...] + (0.05 / BLK) * r_o[...]

    pltpu.make_async_remote_copy(
        scl.at[pl.ds(0, NB - 1)], scl.at[pl.ds(0, NB - 1)], s_s.at[0], s_r.at[0],
        device_id={"fsdp": other}, device_id_type=MESH,
    ).wait()
    for p in range(2):
        pltpu.make_async_remote_copy(
            dsend.at[p, pl.ds(0, NB - 1)], dret.at[p, pl.ds(0, NB - 1)], d_s.at[p], d_r.at[p],
            device_id={"fsdp": other}, device_id_type=MESH,
        ).wait()

    def update(b, carry):
        s = own_ref[b]
        step = 0.2 * scl[s]
        for c in range(CH):
            z = zbuf[b, c] - step * dret[c // 2, s, c % 2].astype(F32)
            x = 0.75 * xbuf[b, c] + 0.25 * z
            z_o[b, c] = z
            x_o[b, c] = x
            y_o[b, c] = (0.1 * z + 0.9 * x).astype(BF16)
        return carry

    lax.fori_loop(0, NB, update, 0, unroll=4)

    pltpu.make_async_remote_copy(
        send.at[pl.ds(0, NB - 1)], held.at[pl.ds(0, NB - 1)], g_s.at[0], g_r.at[0],
        device_id={"fsdp": other}, device_id_type=MESH,
    ).wait_send()
    for chunk in b_ring + g_ring:
        chunk[3]()
    for d in (1, 2, 3):
        p_copy(d).wait_send()


def write_kernel(z, x, y, l, r, z_o, x_o, y_o, l_o, r_o, sem):
    copies = [
        pltpu.make_async_copy(a, b, sem.at[n])
        for n, (a, b) in enumerate(((z, z_o), (x, x_o), (y, y_o), (l, l_o), (r, r_o)))
    ]
    for copy in copies:
        copy.start()
    for copy in copies:
        copy.wait()


def pieces_of(flat):
    return flat[0].reshape(4, 512, 128).transpose(1, 0, 2).reshape(NB, CH, 8, 128)


def flat_of(pieces):
    return pieces.reshape(512, 4, 128).transpose(1, 0, 2).reshape(1, 4, 65536)


def per_device(grad, z_params, x_params, owner, stat_left, stat_right, root_left, root_right):
    smem = pl.BlockSpec(memory_space=pltpu.SMEM)
    vmem = pl.BlockSpec(memory_space=pltpu.VMEM)
    anywhere = pl.BlockSpec(memory_space=pl.ANY)
    shapes = (
        ((NB, CH, 8, 128), F32),
        ((NB, CH, 8, 128), F32),
        ((NB, CH, 8, 128), BF16),
        ((Q, BLK), F32),
        ((Q, BLK), F32),
    )
    dma = pltpu.SemaphoreType.DMA
    results = pl.pallas_call(
        remote_kernel,
        out_shape=tuple(pltpu.VMEM(s, t) for s, t in shapes),
        in_specs=[smem] + [anywhere] * 7,
        out_specs=(vmem,) * 5,
        scratch_shapes=[
            pltpu.VMEM((NB, 32, 128), F32),
            pltpu.VMEM((NB, 32, 128), BF16),
            pltpu.VMEM((NB, 32, 128), BF16),
            pltpu.VMEM((4, Q, BLK), BF16),
            pltpu.VMEM((CH, 4, Q, Q), BF16),
            pltpu.VMEM((4, Q, Q), BF16),
            pltpu.VMEM((Q, BLK), F32),
            pltpu.VMEM((Q, BLK), BF16),
            pltpu.VMEM((NB, CH, 8, 128), F32),
            pltpu.VMEM((NB, CH, 8, 128), F32),
            pltpu.VMEM((Q, BLK), F32),
            pltpu.VMEM((Q, BLK), F32),
            pltpu.VMEM((Q, Q), BF16),
            pltpu.VMEM((Q, Q), BF16),
            pltpu.VMEM((2, NB, 2, 8, 128), BF16),
            pltpu.VMEM((2, NB, 2, 8, 128), BF16),
            pltpu.VMEM((4, 2, 8, 128), F32),
            pltpu.VMEM((NB, 1, 128), F32),
            pltpu.VMEM((1, 128), F32),
            pltpu.VMEM((NB, 128), jnp.int32),
            pltpu.VMEM((1, 128), jnp.int32),
            pltpu.SMEM((1, 128), jnp.int32),
            dma((14,)),
            pltpu.SemaphoreType.REGULAR,
            pltpu.SemaphoreType.REGULAR,
            dma((CH + GC, 2)),
            dma((CH + GC, 2)),
            dma((CH + GC, 2)),
            dma((CH + GC, 2)),
            dma((1,)),
            dma((GC,)),
            dma((2,)),
            dma((2,)),
            dma((3,)),
            dma((3,)),
            dma((1,)),
            dma((1,)),
        ],
        compiler_params=pltpu.CompilerParams(
            collective_id=0, has_side_effects=True, vmem_limit_bytes=57 << 20
        ),
        name="shampoo",
    )(
        owner, pieces_of(grad).reshape(NB, 32, 128), pieces_of(z_params), pieces_of(x_params),
        stat_left[0], stat_right[0], root_left[0], root_right[0],
    )
    z, x, y, left_new, right_new = pl.pallas_call(
        write_kernel,
        out_shape=tuple(jax.ShapeDtypeStruct(s, t) for s, t in shapes),
        in_specs=[vmem] * 5,
        out_specs=(anywhere,) * 5,
        scratch_shapes=[dma((5,))],
        compiler_params=pltpu.CompilerParams(vmem_limit_bytes=8 << 20),
        name="write",
    )(*results)
    return (flat_of(z), flat_of(x), flat_of(y), left_new[None], right_new[None])


def solution(mesh):
    return jax.shard_map(
        per_device,
        mesh=mesh,
        in_specs=(P("rep", "fsdp", None),) * 3 + (P(),) + (P("fsdp", "rep", None),) * 4,
        out_specs=(P("rep", "fsdp", None),) * 3 + (P("fsdp", "rep", None),) * 2,
        check_vma=False,
    )
```

time: 70.5 us -> 65.4 us (0.928)
  Pallas kernels: 68.5 us -> 64.7 us
    pallas_call x1, Pallas kernels: 66.3 us -> 62.4 us  [per_device(): pl.pallas_call(remote_kernel, out_shape=tuple((pltpu.VMEM(s, t) for s, t...]
where the time goes in v3:
time: 65.4 us; the launch traced here: 65.3 us
  Pallas kernels  64.7 us (99%)
    pallas_call x1, Pallas kernels, per_device(): pl.pallas_call(remote_kernel, out_shape=tuple((pltpu.VMEM(s, t) for s, t...  62.4 us
    pallas_call x1, Pallas kernels, per_device(): pl.pallas_call(write_kernel, out_shape=tuple((jax.ShapeDtypeStruct(s, t)...  2.22 us

profile of v3, /device:TPU:1, one launch (start us, length us, event | category | flops | bytes accessed | tf_op | source)
XLA Modules:
  0.0 65.3 jit_solution(12857351749416719850)
XLA Ops:
  0.6 62.4 %shampoo.1 = (f32[64,4,8,128]{3,2,1,0:T(8,128)S(1)}, f32[64,4,8,128]{3,2,1,0:T(8,128)S(1)}, bf16[64,4,8,128]{3,2,1,0:T(8,128)(2,1)S(1)}, f32[256,1024]{1,0:T(8,128)S(1)}, f32[256,1024]{1,0:T(8,128)S(1)}) custom-call(s32[64]{0:T(128)} %own_ref.1, f32[64,32,128]{2,1,0:T(8,128)} %bitcast.36, f32[64,4,8,128]{3,2,1,0:T(8,128)} %bitcast.37, ...), custom_call_target="tpu_custom_call" | custom-call | tf_op jit(solution)/shard_map/shampoo/pallas_call | solution.py:388
  63.1 2.2 %write.1 = (f32[64,4,8,128]{3,2,1,0:T(8,128)}, f32[64,4,8,128]{3,2,1,0:T(8,128)}, bf16[64,4,8,128]{3,2,1,0:T(8,128)(2,1)}, f32[256,1024]{1,0:T(8,128)}, f32[256,1024]{1,0:T(8,128)}) custom-call(f32[64,4,8,128]{3,2,1,0:T(8,128)S(1)} %get-tuple-element.15.z, f32[64,4,8,128]{3,2,1,0:T(8,128)S(1)} %get-tuple-element.16.x, ...), custom_call_target="tpu_custom_call" | custom-call | tf_op jit(solution)/shard_map/write/pallas_call | solution.py:440

commit v4 on v3

--- a/solution.py
+++ b/solution.py
@@ -32,10 +32,10 @@
 
 
 def remote_kernel(
-    own_ref, grad_ref, z_ref, x_ref, sl_ref, sr_ref, rl_ref, rr_ref,
+    own_hbm, grad_ref, z_ref, x_ref, sl_ref, sr_ref, rl_ref, rr_ref,
     z_o, x_o, y_o, l_o, r_o,
     gbuf, send, held, gq, bc, ac, lg, lgb, zbuf, xbuf, slbuf, srbuf,
-    perm1, perm2, dsend, dret, part, scl, sclsend, spread, invv, inv,
+    perm1, perm2, dsend, dret, part, scl, sclsend, spread, invv, inv, own_ref,
     loc, line_sem, core_sem, y_s1, y_s2, y_r1, y_r2, g_s, g_r, d_s, d_r, p_s, p_r, s_s, s_r,
 ):
     f = lax.axis_index("fsdp")
@@ -64,6 +64,8 @@
     for d in (1, 2, 3):
         greet({"fsdp": ((fx + d) % 4) * LINE + fz * 2 + 1, "rep": r})
 
+    owners = pltpu.make_async_copy(own_hbm, own_ref, loc.at[14])
+    owners.start()
     loads = []
     for c in range(CH):
         loads.append(
@@ -78,6 +80,8 @@
         loads.append(pltpu.make_async_copy(a, b, loc.at[9 + n]))
     for load in loads:
         load.start()
+
+    owners.wait()
 
     def spread_row(b, c):
         spread[pl.ds(b, 1), :] = jnp.full((1, 128), own_ref[b], jnp.int32)
@@ -174,7 +178,7 @@
             ).start()
             return c
 
-        lax.fori_loop(1 if q == 0 else 8 * q, 8 * q + 8, body, 0)
+        lax.fori_loop(1 if q == 0 else 8 * q, 8 * q + 8, body, 0, unroll=True)
 
     def g_take(q):
         count = 7 if q == 0 else 8
@@ -207,7 +211,10 @@
     g_send(0)
     g_send(1)
     pl.semaphore_wait(line_sem, 3)
-    for q in range(2, GC):
+    for q in range(2, 5):
+        g_send(q)
+    b_ring[0][1]()
+    for q in range(5, GC):
         g_send(q)
 
     for load in loads[5:]:
@@ -233,7 +240,6 @@
             )
             r_o[:, cols] = term if first else r_o[:, cols] + term
 
-    b_ring[0][1]()
     b_ring[1][1]()
     for q in range(GC):
         g_take(q)
@@ -284,7 +290,7 @@
             ).start()
             return carry
 
-        lax.fori_loop(1, NB, body, 0)
+        lax.fori_loop(1, NB, body, 0, unroll=9)
         dret[p, f] = dsend[p, f]
 
     product(0)
@@ -316,7 +322,7 @@
         ).start()
         return carry
 
-    lax.fori_loop(1, NB, s_start, 0)
+    lax.fori_loop(1, NB, s_start, 0, unroll=9)
     stats(across, False)
     l_o[...] = 0.95 * slbuf[...] + (0.05 / BLK) * l_o[...]
     r_o[...] = 0.95 * srbuf[...] + (0.05 / BLK) * r_o[...]
@@ -374,7 +380,6 @@
 
 
 def per_device(grad, z_params, x_params, owner, stat_left, stat_right, root_left, root_right):
-    smem = pl.BlockSpec(memory_space=pltpu.SMEM)
     vmem = pl.BlockSpec(memory_space=pltpu.VMEM)
     anywhere = pl.BlockSpec(memory_space=pl.ANY)
     shapes = (
@@ -388,7 +393,7 @@
     results = pl.pallas_call(
         remote_kernel,
         out_shape=tuple(pltpu.VMEM(s, t) for s, t in shapes),
-        in_specs=[smem] + [anywhere] * 7,
+        in_specs=[anywhere] * 8,
         out_specs=(vmem,) * 5,
         scratch_shapes=[
             pltpu.VMEM((NB, 32, 128), F32),
@@ -413,7 +418,8 @@
             pltpu.VMEM((NB, 128), jnp.int32),
             pltpu.VMEM((1, 128), jnp.int32),
             pltpu.SMEM((1, 128), jnp.int32),
-            dma((14,)),
+            pltpu.SMEM((NB,), jnp.int32),
+            dma((15,)),
             pltpu.SemaphoreType.REGULAR,
             pltpu.SemaphoreType.REGULAR,
             dma((CH + GC, 2)),

time: 65.4 us -> 64.1 us (0.980)
  Pallas kernels: 64.7 us -> 63.4 us
    pallas_call x1, Pallas kernels: 62.4 us -> 61.2 us  [per_device(): pl.pallas_call(remote_kernel, out_shape=tuple((pltpu.VMEM(s, t) for s, t...]
where the time goes in v4:
time: 64.1 us
  Pallas kernels  63.4 us (99%)
    pallas_call x1, Pallas kernels, per_device(): pl.pallas_call(remote_kernel, out_shape=tuple((pltpu.VMEM(s, t) for s, t...  61.2 us
    pallas_call x1, Pallas kernels, per_device(): pl.pallas_call(write_kernel, out_shape=tuple((jax.ShapeDtypeStruct(s, t)...  2.22 us

profile of v4, /device:TPU:1, one launch (start us, length us, event | category | flops | bytes accessed | tf_op | source)
XLA Modules:
  0.0 64.1 jit_solution(1962462136039652439)
XLA Ops:
  0.6 61.2 %shampoo.1 = (f32[64,4,8,128]{3,2,1,0:T(8,128)S(1)}, f32[64,4,8,128]{3,2,1,0:T(8,128)S(1)}, bf16[64,4,8,128]{3,2,1,0:T(8,128)(2,1)S(1)}, f32[256,1024]{1,0:T(8,128)S(1)}, f32[256,1024]{1,0:T(8,128)S(1)}) custom-call(s32[64]{0:T(128)} %own_hbm.1, f32[64,32,128]{2,1,0:T(8,128)} %bitcast.36, f32[64,4,8,128]{3,2,1,0:T(8,128)} %bitcast.37, ...), custom_call_target="tpu_custom_call" | custom-call | tf_op jit(solution)/shard_map/shampoo/pallas_call | solution.py:393
  61.8 2.2 %write.1 = (f32[64,4,8,128]{3,2,1,0:T(8,128)}, f32[64,4,8,128]{3,2,1,0:T(8,128)}, bf16[64,4,8,128]{3,2,1,0:T(8,128)(2,1)}, f32[256,1024]{1,0:T(8,128)}, f32[256,1024]{1,0:T(8,128)}) custom-call(f32[64,4,8,128]{3,2,1,0:T(8,128)S(1)} %get-tuple-element.15.z, f32[64,4,8,128]{3,2,1,0:T(8,128)S(1)} %get-tuple-element.16.x, ...), custom_call_target="tpu_custom_call" | custom-call | tf_op jit(solution)/shard_map/write/pallas_call | solution.py:446

commit v5 on v4

--- a/solution.py
+++ b/solution.py
@@ -302,8 +302,6 @@
     product(2)
     product(3)
     d_send(1)
-    stats(left, False)
-    stats(right, False)
     for d in (1, 2, 3):
         p_copy(d).wait_recv()
     entries = float(BLK * BLK)
@@ -323,6 +321,8 @@
         return carry
 
     lax.fori_loop(1, NB, s_start, 0, unroll=9)
+    stats(left, False)
+    stats(right, False)
     stats(across, False)
     l_o[...] = 0.95 * slbuf[...] + (0.05 / BLK) * l_o[...]
     r_o[...] = 0.95 * srbuf[...] + (0.05 / BLK) * r_o[...]

time: 64.1 us -> 64.1 us (level)
  no operation moved by 1% of the time
where the time goes in v5:
time: 64.1 us; the launch traced here: 64 us
  Pallas kernels  63.4 us (99%)
    pallas_call x1, Pallas kernels, per_device(): pl.pallas_call(remote_kernel, out_shape=tuple((pltpu.VMEM(s, t) for s, t...  61.2 us
    pallas_call x1, Pallas kernels, per_device(): pl.pallas_call(write_kernel, out_shape=tuple((jax.ShapeDtypeStruct(s, t)...  2.22 us

profile of v5, /device:TPU:1, one launch (start us, length us, event | category | flops | bytes accessed | tf_op | source)
XLA Modules:
  0.0 64.0 jit_solution(8980324935064296803)
XLA Ops:
  0.6 61.2 %shampoo.1 = (f32[64,4,8,128]{3,2,1,0:T(8,128)S(1)}, f32[64,4,8,128]{3,2,1,0:T(8,128)S(1)}, bf16[64,4,8,128]{3,2,1,0:T(8,128)(2,1)S(1)}, f32[256,1024]{1,0:T(8,128)S(1)}, f32[256,1024]{1,0:T(8,128)S(1)}) custom-call(s32[64]{0:T(128)} %own_hbm.1, f32[64,32,128]{2,1,0:T(8,128)} %bitcast.36, f32[64,4,8,128]{3,2,1,0:T(8,128)} %bitcast.37, ...), custom_call_target="tpu_custom_call" | custom-call | tf_op jit(solution)/shard_map/shampoo/pallas_call | solution.py:393
  61.8 2.2 %write.1 = (f32[64,4,8,128]{3,2,1,0:T(8,128)}, f32[64,4,8,128]{3,2,1,0:T(8,128)}, bf16[64,4,8,128]{3,2,1,0:T(8,128)(2,1)}, f32[256,1024]{1,0:T(8,128)}, f32[256,1024]{1,0:T(8,128)}) custom-call(f32[64,4,8,128]{3,2,1,0:T(8,128)S(1)} %get-tuple-element.15.z, f32[64,4,8,128]{3,2,1,0:T(8,128)S(1)} %get-tuple-element.16.x, ...), custom_call_target="tpu_custom_call" | custom-call | tf_op jit(solution)/shard_map/write/pallas_call | solution.py:446
